TPU v7x, 32 devices: a whole 2x2x4 slice. The times are simulated.
32 devices in a mesh: groups: 1, rows: 16 (over z, y, core), heads: 2 (over x).
Axes of the slice: x: 2, y: 2, z: 4, core: 2. Of those that a mesh axis runs over, the one named last changes fastest.
Arguments:
- queries: bfloat16 [2048, 8192], P(('groups', 'rows'), 'heads'), may hold values from -40 to 40
- passages: bfloat16 [768, 1024], P(('groups', 'rows')), may hold values from -6 to 6
- enc_gain: bfloat16 [1024], replicated, may hold values from 0.099609375 to 1.8984375
- key_weight: bfloat16 [1024, 8192], P(None, 'heads'), may hold values from -0.1875 to 0.1875
- value_weight: bfloat16 [1024, 8192], P(None, 'heads'), may hold values from -0.1875 to 0.1875
- out_weight: bfloat16 [8192, 1024], P('heads'), may hold values from -0.125 to 0.125
- passage_length: int32 [3], P('groups'), may hold values from 64 to 256, as said below
Outputs:
- cross_out: bfloat16 [2048, 1024], P(('groups', 'rows'))
Inputs may be any that keep to these rules, and one draw needn't show every extreme that they name: `passage_length`: every passage has at least a quarter of its padded tokens; some passage is full and some has exactly 64 tokens.
All inputs are finite; a program needn't handle non-finite values.
Results may differ from a plain program's by a relative error of at most 0.012.
The roundings to bfloat16 on the way count: a program that leaves them out, or rounds other values in their place, can miss the bound.
Values may be sent and summed in bfloat16 or wider, within the bound.
No kernel may reach another device: no remote copies, remote signals or barrier semaphores. Data moves between devices by JAX's collectives and lax.ppermute only.
A program may use at most 128 MiB of HBM per device.

v0:
```python
import functools

import jax
import jax.numpy as jnp
from jax import lax
from jax.experimental import pallas as pl
from jax.experimental.pallas import tpu as pltpu
from jax.sharding import PartitionSpec as P

DK = 128
PASS_LEN = 256
LOWEST = -1e30
TILE = 16
WIDE = 1024
ON_CHIP = pl.BlockSpec(memory_space=pltpu.VMEM)
SCALARS = pl.BlockSpec(memory_space=pltpu.SMEM)
FAR = pl.BlockSpec(memory_space=pltpu.HBM)


def params(mib):
    return pltpu.CompilerParams(vmem_limit_bytes=mib * 1024 * 1024)


def cost(flops, moved, exps=0):
    return pl.CostEstimate(flops=flops, bytes_accessed=moved, transcendentals=exps)


def chip_cycle(chips):
    up = list(range(0, chips, 2))
    return up + [chip for chip in range(chips - 1, -1, -1) if chip % 2]


def owner_of(device, source, chips):
    offset, crossed = source
    chip, core = device >> 1, device & 1
    place = jnp.where((chip & 1) == 0, chip >> 1, chips - ((chip + 1) >> 1)) + offset
    place = jnp.where(place < 0, place + chips, jnp.where(place >= chips, place - chips, place))
    chip = jnp.where(place < (chips + 1) >> 1, place << 1, ((chips - place) << 1) - 1)
    return (chip << 1) + (core ^ crossed)


class Plan:
    def __init__(self, order, rows_piece, passages):
        self.order, self.per_piece = order, rows_piece // TILE
        self.rows_piece, self.passages = rows_piece, passages
        self.tiles = len(order) * self.per_piece
        self.size = 2 * self.tiles + 2 + passages

    def write(self, plan, device, length_ref, chips):
        shift = PASS_LEN.bit_length() - 1
        for passage in range(self.passages):
            plan[2 * self.tiles + 2 + passage] = -1
        kept = jnp.int32(0)
        for index, source in enumerate(self.order):
            first = owner_of(device, source, chips) * self.rows_piece
            for tile in range(index * self.per_piece, (index + 1) * self.per_piece):
                row = first + (tile - index * self.per_piece) * TILE
                passage = row >> shift
                here = length_ref[passage] - (row & (PASS_LEN - 1))
                plan[tile] = here
                plan[self.tiles + tile] = kept

                @pl.when((here > 0) & (here < TILE))
                def _(kept=kept, here=here, passage=passage):
                    plan[2 * self.tiles + 2 + passage] = kept * TILE + here

                kept = kept + (here > 0).astype(jnp.int32)
        plan[2 * self.tiles] = kept
        plan[2 * self.tiles + 1] = device & 1

    def here(self, plan, tile):
        return plan[tile]

    def place(self, plan, tile):
        return plan[self.tiles + tile]

    def total(self, plan):
        return plan[2 * self.tiles]

    def core(self, plan):
        return plan[2 * self.tiles + 1]

    def partial(self, plan, passage):
        return plan[2 * self.tiles + 2 + passage]


def keep_valid(layout, plan, first, piece_refs, raw):
    begin = layout.place(plan, first * layout.per_piece)
    after = (first + len(piece_refs)) * layout.per_piece
    for index, piece_ref in enumerate(piece_refs):
        for tile in range(layout.per_piece):
            at = (first + index) * layout.per_piece + tile

            @pl.when(layout.here(plan, at) > 0)
            def _(at=at, tile=tile, piece_ref=piece_ref):
                row = pl.multiple_of((layout.place(plan, at) - begin) * TILE, TILE)
                raw[pl.ds(row, TILE), :] = piece_ref[tile * TILE:(tile + 1) * TILE, :]

    end = layout.place(plan, after) if after < layout.tiles else layout.total(plan)
    return begin, end - begin


def normalize(raw, rows, gain_ref, kept, number):
    wide = raw[:number, :].astype(jnp.float32)
    mean_square = jnp.mean(wide * wide, axis=-1, keepdims=True)
    scaled = wide * lax.rsqrt(mean_square + 1e-06) * gain_ref[...].astype(jnp.float32).reshape(1, -1)
    row = lax.broadcasted_iota(jnp.int32, scaled.shape, 0)
    rows[:number, :] = jnp.where(row < kept * TILE, scaled, 0.0).astype(jnp.bfloat16)


def stage_kernel(axis, device_ref, far, near, sem):
    half = near.shape[axis]
    ours = pl.ds(pl.multiple_of((device_ref[0] & 1) * half, half), half)
    copy = pltpu.make_async_copy(far.at[(slice(None),) * axis + (ours,)], near, sem)
    copy.start()
    copy.wait()


def stage(device, weight, axis):
    shape = tuple(size // 2 if at == axis else size for at, size in enumerate(weight.shape))
    return pl.pallas_call(
        functools.partial(stage_kernel, axis),
        in_specs=[SCALARS, FAR],
        out_specs=ON_CHIP,
        out_shape=jax.ShapeDtypeStruct(shape, weight.dtype),
        scratch_shapes=[pltpu.SemaphoreType.DMA],
        compiler_params=params(48),
        cost_estimate=cost(0, 2 * weight.size),
        name="stage",
    )(device, weight)


def write_mask(layout, plan, mask_ref):
    row = lax.broadcasted_iota(jnp.int32, mask_ref.shape, 0)
    valid = row < layout.total(plan) * TILE
    for passage in range(layout.passages):
        begin = layout.partial(plan, passage)
        end = ((begin + TILE - 1) >> (TILE.bit_length() - 1)) * TILE
        valid = valid & ((begin < 0) | (row < begin) | (row >= end))
    first_column = lax.broadcasted_iota(jnp.int32, mask_ref.shape, 1) == 0
    mask_ref[...] = jnp.where(first_column & ~valid, LOWEST, 0.0).astype(jnp.bfloat16)


def begin_kernel(layout, chips, device_ref, length_far, gain_far, key_w_ref, value_far, queries_far, own_far,
                 crossed_ref, plan, gain_ref, value_w_ref, keys_ref, values_ref, own_q_ref, given_q_ref, mask_ref,
                 length_ref, own_ref, raw, rows, sems):
    device = device_ref[0]
    half = value_w_ref.shape[1]
    ours = pl.ds(pl.multiple_of((device & 1) * half, half), half)
    theirs = pl.ds(pl.multiple_of((1 - (device & 1)) * half, half), half)
    moves = (
        (length_far, length_ref),
        (own_far, own_ref),
        (gain_far, gain_ref),
        (value_far.at[:, ours], value_w_ref),
        (queries_far.at[:, ours], own_q_ref),
        (queries_far.at[:, theirs], given_q_ref),
    )
    copies = [
        pltpu.make_async_copy(source, target, sems.at[index])
        for index, (source, target) in enumerate(moves)
    ]
    for copy in copies:
        copy.start()
    copies[0].wait()
    layout.write(plan, device, length_ref, chips)
    copies[1].wait()
    _, kept = keep_valid(layout, plan, 0, [own_ref, crossed_ref], raw)
    copies[2].wait()
    number = raw.shape[0]
    normalize(raw, rows, gain_ref, kept, number)
    for weight_ref, out_ref in ((key_w_ref, keys_ref), (value_w_ref, values_ref)):
        if weight_ref is value_w_ref:
            write_mask(layout, plan, mask_ref)
            for copy in copies[3:]:
                copy.wait()
        for left in range(0, half, WIDE):
            columns = slice(left, min(left + WIDE, half))
            out_ref[:number, columns] = jnp.dot(
                rows[...], weight_ref[:, columns], preferred_element_type=jnp.float32
            ).astype(jnp.bfloat16)


def begin(layout, chips, device, passage_length, gain, key_w, value_weight, queries, own, crossed, held_rows):
    width, half = key_w.shape
    held = jax.ShapeDtypeStruct((held_rows, half), jnp.bfloat16)
    query_half = jax.ShapeDtypeStruct((queries.shape[0], half), queries.dtype)
    return pl.pallas_call(
        functools.partial(begin_kernel, layout, chips),
        in_specs=[SCALARS, FAR, FAR, ON_CHIP, FAR, FAR, FAR, ON_CHIP],
        out_specs=[SCALARS] + [ON_CHIP] * 7,
        out_shape=[
            jax.ShapeDtypeStruct((layout.size,), jnp.int32),
            jax.ShapeDtypeStruct(gain.shape, gain.dtype),
            jax.ShapeDtypeStruct(key_w.shape, key_w.dtype),
            held, held, query_half, query_half,
            jax.ShapeDtypeStruct((layout.tiles * TILE, DK), jnp.bfloat16),
        ],
        scratch_shapes=[
            pltpu.SMEM(passage_length.shape, jnp.int32),
            pltpu.VMEM(own.shape, own.dtype),
            pltpu.VMEM((2 * own.shape[0], width), jnp.bfloat16),
            pltpu.VMEM((2 * own.shape[0], width), jnp.bfloat16),
            pltpu.SemaphoreType.DMA((6,)),
        ],
        compiler_params=params(36),
        cost_estimate=cost(8 * own.shape[0] * width * half, 8 * width * half),
        name="begin",
    )(device, passage_length, gain, key_w, value_weight, queries, own, crossed)


def append(layout, first, cases, plan, piece_refs, gain_ref, key_w_ref, value_w_ref, keys_ref, values_ref, raw, rows):
    begin_tile, kept = keep_valid(layout, plan, first, piece_refs, raw)
    start = pl.multiple_of(begin_tile * TILE, TILE)
    width = key_w_ref.shape[1]

    def project(number):
        normalize(raw, rows, gain_ref, kept, number)
        for left in range(0, width, WIDE):
            columns = slice(left, min(left + WIDE, width))
            for weight_ref, out_ref in ((key_w_ref, keys_ref), (value_w_ref, values_ref)):
                out_ref[pl.ds(start, number), columns] = jnp.dot(
                    rows[:number, :], weight_ref[:, columns], preferred_element_type=jnp.float32
                ).astype(jnp.bfloat16)

    low = 0
    for number in cases:
        pl.when((kept * TILE > low) & (kept * TILE <= number))(functools.partial(project, number))
        low = number


def cases_of(rows_now):
    return list(range(rows_now, rows_now // 3, -64))[::-1]


def project_kernel(layout, first, count, cases, stages, plan, gain_ref, key_w_ref, value_w_ref, *refs):
    piece_refs = refs[:count]
    if stages:
        out_far, out_w_ref, sem = refs[count], refs[-4], refs[-1]
        refs = refs[:-4] + refs[-3:-1]
        half = out_w_ref.shape[0]
        ours = pl.ds(pl.multiple_of(layout.core(plan) * half, half), half)
        staging = pltpu.make_async_copy(out_far.at[ours, :], out_w_ref, sem)
        staging.start()
    keys_ref, values_ref, raw, rows = refs[-4:]
    append(layout, first, cases, plan, piece_refs, gain_ref, key_w_ref, value_w_ref, keys_ref, values_ref, raw, rows)
    if stages:
        staging.wait()


def project(layout, first, plan, gain, key_w, value_w, pieces, held, out_weight=None):
    rows_now = len(pieces) * layout.rows_piece
    width, half = key_w.shape
    stages = out_weight is not None
    shapes = [jax.ShapeDtypeStruct(held[0].shape, jnp.bfloat16)] * 2
    if stages:
        shapes.append(jax.ShapeDtypeStruct((half, out_weight.shape[1]), out_weight.dtype))
    at = 4 + len(pieces) + stages
    return pl.pallas_call(
        functools.partial(project_kernel, layout, first, len(pieces), cases_of(rows_now), stages),
        in_specs=[SCALARS] + [ON_CHIP] * (3 + len(pieces)) + [FAR] * stages + [ON_CHIP] * 2,
        out_specs=[ON_CHIP] * len(shapes),
        out_shape=shapes,
        scratch_shapes=[pltpu.VMEM((rows_now, width), jnp.bfloat16)] * 2 + [pltpu.SemaphoreType.DMA] * stages,
        input_output_aliases={at: 0, at + 1: 1},
        compiler_params=params(28 if stages else 16),
        cost_estimate=cost(4 * rows_now * width * half, 4 * width * half),
        name="project",
    )(plan, gain, key_w, value_w, *pieces, *([out_weight] if stages else []), *held)


def attend_kernel(layout, first, count, cases, plan, gain_ref, key_w_ref, value_w_ref, mask, own_q_ref, other_q_ref,
                  out_w_ref, *refs):
    piece_refs = refs[:count]
    own_ref, other_ref, keys_ref, values_ref, raw, rows = refs[count + 2:]
    append(layout, first, cases_of(raw.shape[0]), plan, piece_refs, gain_ref, key_w_ref, value_w_ref,
           keys_ref, values_ref, raw, rows)
    half, inner = own_q_ref.shape
    heads = inner // DK
    kept = layout.total(plan)

    def attend(number):
        def clear(tile, carry):
            at = pl.ds(pl.multiple_of(tile * TILE, TILE), TILE)
            keys_ref[at, :] = jnp.zeros((TILE, inner), jnp.bfloat16)
            values_ref[at, :] = jnp.zeros((TILE, inner), jnp.bfloat16)
            return carry

        lax.fori_loop(kept, number // TILE, clear, 0)
        ones = jnp.where(
            lax.broadcasted_iota(jnp.int32, (2 * half, DK), 1) == 0, 1.0, 0.0
        ).astype(jnp.bfloat16)

        def scores_of(head):
            here = slice(head * DK, (head + 1) * DK)
            query_rows = jnp.concatenate([own_q_ref[:, here], other_q_ref[:, here]], axis=0)
            return lax.dot_general(
                jnp.concatenate([query_rows, ones], axis=1),
                jnp.concatenate([keys_ref[:number, here], mask[:number, :]], axis=1),
                (((1,), (1,)), ((), ())), preferred_element_type=jnp.float32,
            )

        def weigh(scores):
            expo = jnp.exp(scores - jnp.max(scores, axis=-1, keepdims=True))
            return expo.astype(jnp.bfloat16), jnp.sum(expo, axis=-1, keepdims=True)

        def mix(head, weights, denom):
            mixed = jnp.dot(
                weights, values_ref[:number, head * DK:(head + 1) * DK],
                preferred_element_type=jnp.float32,
            )
            return (mixed * (1.0 / denom)).astype(jnp.bfloat16)

        attended, scores, weighed = [], scores_of(0), None
        for head in range(heads):
            ahead = scores_of(head + 1) if head + 1 < heads else None
            weighing = weigh(scores)
            if weighed is not None:
                attended.append(mix(head - 1, *weighed))
            scores, weighed = ahead, weighing
        attended.append(mix(heads - 1, *weighed))
        product = jnp.dot(
            jnp.concatenate(attended, axis=1), out_w_ref[...], preferred_element_type=jnp.float32
        )
        own_ref[...] = product[:half, :].astype(jnp.bfloat16)
        other_ref[...] = product[half:, :].astype(jnp.bfloat16)

    low = 0
    for number in cases:
        pl.when((kept * TILE > low) & (kept * TILE <= number))(functools.partial(attend, number))
        low = number


def attend(layout, first, plan, gain, key_w, value_w, mask, own_q, other_q, out_w, pieces, held):
    rows_here, half = own_q.shape
    width = out_w.shape[1]
    enc_rows = layout.tiles * TILE
    cases = [enc_rows * 2 // 3 // 64 * 64, enc_rows]
    result = jax.ShapeDtypeStruct((rows_here, width), jnp.bfloat16)
    kept = jax.ShapeDtypeStruct(held[0].shape, jnp.bfloat16)
    at = 8 + len(pieces)
    own, other, _, _ = pl.pallas_call(
        functools.partial(attend_kernel, layout, first, len(pieces), cases),
        in_specs=[SCALARS] + [ON_CHIP] * (at + 1),
        out_specs=[ON_CHIP] * 4,
        out_shape=[result, result, kept, kept],
        scratch_shapes=[pltpu.VMEM((len(pieces) * layout.rows_piece, width), jnp.bfloat16)] * 2,
        input_output_aliases={at: 2, at + 1: 3},
        compiler_params=params(24),
        cost_estimate=cost(4 * rows_here * (2 * enc_rows + width) * half, 2 * half * width),
        name="attend",
    )(plan, gain, key_w, value_w, mask, own_q, other_q, out_w, *pieces, *held)
    return own, other


def on_device(number, queries, passages, enc_gain, key_weight, value_weight, out_weight, passage_length):
    rows_piece = passages.shape[0]
    heads_axis = lax.axis_size("heads")
    chips = number // 2
    cycle = chip_cycle(chips)
    place = {chip: index for index, chip in enumerate(cycle)}
    other_core = [(device, device ^ 1) for device in range(number)]

    def hop(by, crossed=0):
        return [
            (2 * chip + core, 2 * cycle[(place[chip] + by) % chips] + (core ^ crossed))
            for chip in range(chips)
            for core in range(2)
        ]

    def cross(piece):
        return lax.ppermute(piece, "rows", other_core)

    rounds = []
    for distance in range(1, chips // 2 + 1):
        if 2 * distance == chips:
            rounds.append([(-distance, 0), (distance, 1)])
        else:
            rounds.append([(-distance, 0), (distance, 0), (-distance, 1), (distance, 1)])
    order = [(0, 0), (0, 1)] + [source for sources in rounds for source in sources]
    layout = Plan(order, rows_piece, passage_length.shape[0])

    device = lax.axis_index("rows").reshape(1)
    held_rows = number * rows_piece
    crossed = cross(passages)
    ahead = behind = passages
    first, waiting, held, out_w = 2, [], [], None
    for index, sources in enumerate(rounds):
        ahead = lax.ppermute(ahead, "rows", hop(1))
        behind = lax.ppermute(behind, "rows", hop(-1, 1 if len(sources) == 2 else 0))
        if index == 0:
            key_w = stage(device, key_weight, 1)
            ahead, behind, key_w = lax.optimization_barrier((ahead, behind, key_w))
        if index == min(1, len(rounds) - 1):
            plan, gain, value_w, keys, values, own_q, given_q, mask = begin(
                layout, chips, device, passage_length, enc_gain, key_w, value_weight,
                queries, passages, crossed, held_rows,
            )
            held = [keys, values]
        elif index > 1:
            last = index == len(rounds) - 1
            now = len(waiting) if last else 6
            *held, staged = project(
                layout, first, plan, gain, key_w, value_w, waiting[:now], held, out_weight if last else None
            )
            if last:
                out_w = staged
            else:
                held.append(staged)
            first, waiting = first + now, waiting[now:]
        ahead, behind, *held = lax.optimization_barrier((ahead, behind, *held))
        waiting = waiting + ([ahead, behind] if len(sources) == 2 else [ahead, behind, cross(ahead), cross(behind)])
    if out_w is None:
        out_w = stage(device, out_weight, 0)
    other_q = cross(given_q)

    own, other = attend(
        layout, first, plan, gain, key_w, value_w, mask, own_q, other_q, out_w, waiting, held
    )
    share = (own.astype(jnp.float32) + cross(other).astype(jnp.float32)).astype(jnp.bfloat16)
    by = 1
    while by < heads_axis:
        turn = [(place, place ^ by) for place in range(heads_axis)]
        given = lax.ppermute(share, "heads", turn)
        share = (share.astype(jnp.float32) + given.astype(jnp.float32)).astype(jnp.bfloat16)
        by *= 2
    return share


def solution(mesh):
    return jax.shard_map(
        functools.partial(on_device, mesh.shape["rows"]),
        mesh=mesh,
        in_specs=(
            P(("groups", "rows"), "heads"),
            P(("groups", "rows"), None),
            P(),
            P(None, "heads"),
            P(None, "heads"),
            P("heads", None),
            P("groups"),
        ),
        out_specs=P(("groups", "rows"), None),
        check_vma=False,
    )
```

profile of v0, /device:TPU:0, one launch (start us, length us, event | category | flops | bytes accessed | tf_op | source)
XLA Modules:
  0.0 45.6 jit_solution(1896220311955892011)
XLA Ops:
  0.0 3.0 %collective-permute-start = (bf16[48,1024]{1,0:T(8,128)(2,1)}, bf16[48,1024]{1,0:T(8,128)(2,1)S(1)}, u32[]{:S(2)}, u32[]{:S(2)}) collective-permute-start(bf16[48,1024]{1,0:T(8,128)(2,1)} %own_far.1), channel_id=1, source_target_pairs={{0,8},{2,10},{4,0},{6,2},{8,16},{10,18},{12,4},{14,6},{16,24},{18,... | collective-permute-start | bytes 294920 | tf_op jit(solution)/shard_map/ppermute | solution.py:389
  3.1 2.3 %stage.1.key_w_ref = bf16[1024,2048]{1,0:T(8,128)(2,1)S(1)} custom-call(s32[1]{0:T(128)} %bitcast.device_ref, bf16[1024,4096]{1,0:T(8,128)(2,1)} %far.1), custom_call_target="tpu_custom_call" | custom-call | bytes 8388608 | tf_op jit(solution)/shard_map/stage/pallas_call | solution.py:121
  5.4 0.6 %collective-permute-done.refs_0_ = bf16[48,1024]{1,0:T(8,128)(2,1)S(1)} collective-permute-done((bf16[48,1024]{1,0:T(8,128)(2,1)}, bf16[48,1024]{1,0:T(8,128)(2,1)S(1)}, u32[]{:S(2)}, u32[]{:S(2)}) %collective-permute-start) | collective-permute-done | bytes 98336 | tf_op jit(solution)/shard_map/ppermute | solution.py:389
  6.0 1.9 %collective-permute-done.1.refs_1_ = bf16[48,1024]{1,0:T(8,128)(2,1)S(1)} collective-permute-done((bf16[48,1024]{1,0:T(8,128)(2,1)}, bf16[48,1024]{1,0:T(8,128)(2,1)S(1)}, u32[]{:S(2)}, u32[]{:S(2)}) %collective-permute-start.1) | collective-permute-done | bytes 98336 | tf_op jit(solution)/shard_map/ppermute | solution.py:390
  7.9 1.6 %collective-permute-start.4 = (bf16[48,1024]{1,0:T(8,128)(2,1)S(1)}, bf16[48,1024]{1,0:T(8,128)(2,1)S(1)}, u32[]{:S(2)}, u32[]{:S(2)}) collective-permute-start(bf16[48,1024]{1,0:T(8,128)(2,1)S(1)} %collective-permute-done.refs_0_), channel_id=1, source_target_pairs={{0,8},{2,10},{4,0},{6,2},{8,16},{10,18},{12,4},{14,6},{16,24},{18,... | collective-permute-start | bytes 294920 | tf_op jit(solution)/shard_map/ppermute | solution.py:389
  9.4 0.4 collective-permute-start.5
  9.9 0.5 %collective-permute-start.11 = (bf16[48,1024]{1,0:T(8,128)(2,1)S(1)}, bf16[48,1024]{1,0:T(8,128)(2,1)S(1)}, u32[]{:S(2)}, u32[]{:S(2)}) collective-permute-start(bf16[48,1024]{1,0:T(8,128)(2,1)S(1)} %collective-permute-done.1.refs_1_), channel_id=1, source_target_pairs={{0,2},{2,0},{4,6},{6,4},{8,10},{10,8},{12,14},{14,12},{16,18},{18,... | collective-permute-start | bytes 294920 | tf_op jit(solution)/shard_map/ppermute | solution.py:372
  10.4 0.0 collective-permute-done.2.crossed_ref
  10.4 3.3 %begin.1 = (s32[101]{0:T(128)S(1)}, bf16[1024]{0:T(1024)(128)(2,1)S(1)}, bf16[1024,2048]{1,0:T(8,128)(2,1)S(1)}, bf16[768,2048]{1,0:T(8,128)(2,1)S(1)}, bf16[768...) custom-call(s32[1]{0:T(128)} %bitcast.device_ref, ...), custom_call_target="tpu_custom_call" | custom-call | flops 805306368 | bytes 16777216 | tf_op jit(solution)/shard_map/begin/pallas_call | solution.py:188
  13.7 0.1 collective-permute-start.3
  13.8 0.2 collective-permute-done.5.refs_5_
  14.0 1.6 %collective-permute-start.8 = (bf16[48,1024]{1,0:T(8,128)(2,1)S(1)}, bf16[48,1024]{1,0:T(8,128)(2,1)S(1)}, u32[]{:S(2)}, u32[]{:S(2)}) collective-permute-start(bf16[48,1024]{1,0:T(8,128)(2,1)S(1)} %collective-permute-done.4.refs_4_), channel_id=1, source_target_pairs={{0,8},{2,10},{4,0},{6,2},{8,16},{10,18},{12,4},{14,6},{16,24},{18,... | collective-permute-start | bytes 294920 | tf_op jit(solution)/shard_map/ppermute | solution.py:389
  15.6 0.0 collective-permute-start.6
  15.6 0.0 collective-permute-done.10.refs_2_
  15.6 0.5 collective-permute-start.9
  16.1 0.2 collective-permute-start.7
  16.3 3.6 %project.2 = (bf16[768,2048]{1,0:T(8,128)(2,1)S(1)}, bf16[768,2048]{1,0:T(8,128)(2,1)S(1)}) custom-call(s32[101]{0:T(128)S(1)} %get-tuple-element.38.plan, bf16[1024]{0:T(1024)(128)(2,1)S(1)} %get-tuple-element.39.gain_ref, bf16[1024,2048]{1,0:T(8,128)(2,1)S(1)} %stage.1.key_w_ref, ...), custom_call_target="tpu_custom_call", output_to_operand_aliasing={{0}: (10, {}), {1}: (11, {})} | custom-call | flops 2415919104 | bytes 8388608 | tf_op jit(solution)/shard_map/project/pallas_call | solution.py:259
  19.9 0.0 collective-permute-done.8.refs_2_
  19.9 0.9 %collective-permute-done.9.refs_3_ = bf16[48,1024]{1,0:T(8,128)(2,1)S(1)} collective-permute-done((bf16[48,1024]{1,0:T(8,128)(2,1)S(1)}, bf16[48,1024]{1,0:T(8,128)(2,1)S(1)}, u32[]{:S(2)}, u32[]{:S(2)}) %collective-permute-start.9) | collective-permute-done | bytes 98336 | tf_op jit(solution)/shard_map/ppermute | solution.py:390
  20.8 0.0 collective-permute-start.12
  20.8 0.5 %collective-permute-start.13 = (bf16[48,1024]{1,0:T(8,128)(2,1)S(1)}, bf16[48,1024]{1,0:T(8,128)(2,1)S(1)}, u32[]{:S(2)}, u32[]{:S(2)}) collective-permute-start(bf16[48,1024]{1,0:T(8,128)(2,1)S(1)} %collective-permute-done.9.refs_3_), channel_id=1, source_target_pairs={{0,2},{2,0},{4,6},{6,4},{8,10},{10,8},{12,14},{14,12},{16,18},{18,... | collective-permute-start | bytes 294920 | tf_op jit(solution)/shard_map/ppermute | solution.py:372
  21.4 1.5 %collective-permute-start.14 = (bf16[48,1024]{1,0:T(8,128)(2,1)S(1)}, bf16[48,1024]{1,0:T(8,128)(2,1)S(1)}, u32[]{:S(2)}, u32[]{:S(2)}) collective-permute-start(bf16[48,1024]{1,0:T(8,128)(2,1)S(1)} %collective-permute-done.8.refs_2_), channel_id=1, source_target_pairs={{0,8},{2,10},{4,0},{6,2},{8,16},{10,18},{12,4},{14,6},{16,24},{18,... | collective-permute-start | bytes 294920 | tf_op jit(solution)/shard_map/ppermute | solution.py:389
  22.9 2.7 %project.3 = (bf16[768,2048]{1,0:T(8,128)(2,1)S(1)}, bf16[768,2048]{1,0:T(8,128)(2,1)S(1)}, bf16[2048,1024]{1,0:T(8,128)(2,1)S(1)}) custom-call(s32[101]{0:T(128)S(1)} %get-tuple-element.38.plan, bf16[1024]{0:T(1024)(128)(2,1)S(1)} %get-tuple-element.39.gain_ref, ...), custom_call_target="tpu_custom_call", output_to_operand_aliasing={{0}: (11, {}), {1}: (12, {})} | custom-call | flops 2415919104 | bytes 8388608 | tf_op jit(solution)/shard_map/project/pallas_call | solution.py:259
  25.6 0.4 collective-permute-done.14.refs_0_
  26.1 1.9 %collective-permute-done.15.refs_1_ = bf16[48,1024]{1,0:T(8,128)(2,1)S(1)} collective-permute-done((bf16[48,1024]{1,0:T(8,128)(2,1)S(1)}, bf16[48,1024]{1,0:T(8,128)(2,1)S(1)}, u32[]{:S(2)}, u32[]{:S(2)}) %collective-permute-start.15) | collective-permute-done | bytes 98336 | tf_op jit(solution)/shard_map/ppermute | solution.py:390
  27.9 6.8 %attend.1 = (bf16[128,1024]{1,0:T(8,128)(2,1)S(1)}, bf16[128,1024]{1,0:T(8,128)(2,1)S(1)}, bf16[768,2048]{1,0:T(8,128)(2,1)S(1)}, bf16[768,2048]{1,0:T(8,128)(2,1)S(1)}) custom-call(s32[101]{0:T(128)S(1)} %get-tuple-element.38.plan, bf16[1024]{0:T(1024)(128)(2,1)S(1)} %get-tuple-element.39.gain_ref, ...), custom_call_target="tpu_custom_call", output_to_operand_aliasing={{2}: (10, {}), {3}: (11, {})} | custom-call | flops 2684354560 | bytes 4194304 | tf_op jit(solution)/shard_map/attend/pallas_call | solution.py:342
  34.8 0.1 collective-permute-start.16
  34.9 1.5 %collective-permute-done.16 = bf16[128,1024]{1,0:T(8,128)(2,1)S(1)} collective-permute-done((bf16[128,1024]{1,0:T(8,128)(2,1)S(1)}, bf16[128,1024]{1,0:T(8,128)(2,1)S(1)}, u32[]{:S(2)}, u32[]{:S(2)}) %collective-permute-start.16) | collective-permute-done | bytes 262176 | tf_op jit(solution)/shard_map/ppermute | solution.py:372
  36.4 0.1 add_convert_fusion.1
  36.4 1.6 %collective-permute-start.17 = (bf16[128,1024]{1,0:T(8,128)(2,1)S(1)}, bf16[128,1024]{1,0:T(8,128)(2,1)S(1)}, u32[]{:S(2)}, u32[]{:S(2)}) collective-permute-start(bf16[128,1024]{1,0:T(8,128)(2,1)S(1)} %add_convert_fusion.1), channel_id=1, source_target_pairs={{0,1},{1,0},{2,3},{3,2},{4,5},{5,4},{6,7},{7,6},{8,9},{9,8},{10,11... | collective-permute-start | bytes 786440 | tf_op jit(solution)/shard_map/ppermute | solution.py:424
  38.0 6.9 %collective-permute-done.17 = bf16[128,1024]{1,0:T(8,128)(2,1)S(1)} collective-permute-done((bf16[128,1024]{1,0:T(8,128)(2,1)S(1)}, bf16[128,1024]{1,0:T(8,128)(2,1)S(1)}, u32[]{:S(2)}, u32[]{:S(2)}) %collective-permute-start.17) | collective-permute-done | bytes 262176 | tf_op jit(solution)/shard_map/ppermute | solution.py:424
  44.8 0.8 %add_convert_fusion = bf16[128,1024]{1,0:T(8,128)(2,1)} fusion(bf16[128,1024]{1,0:T(8,128)(2,1)S(1)} %collective-permute-done.17, bf16[128,1024]{1,0:T(8,128)(2,1)S(1)} %add_convert_fusion.1), kind=kLoop, calls=%fused_computation | loop fusion | flops 524288 | bytes 786432 | tf_op jit(solution)/shard_map/convert_element_type | solution.py:425
  (19 shorter events, 0.0 us)
Async XLA Ops:
  0.0 6.0 %collective-permute-start = (bf16[48,1024]{1,0:T(8,128)(2,1)}, bf16[48,1024]{1,0:T(8,128)(2,1)S(1)}, u32[]{:S(2)}, u32[]{:S(2)}) collective-permute-start(bf16[48,1024]{1,0:T(8,128)(2,1)} %own_far.1), channel_id=1, source_target_pairs={{0,8},{2,10},{4,0},{6,2},{8,16},{10,18},{12,4},{14,6},{16,24},{18,... | collective-permute-start | bytes 294920 | tf_op jit(solution)/shard_map/ppermute | solution.py:389
  3.0 4.8 %collective-permute-start.1 = (bf16[48,1024]{1,0:T(8,128)(2,1)}, bf16[48,1024]{1,0:T(8,128)(2,1)S(1)}, u32[]{:S(2)}, u32[]{:S(2)}) collective-permute-start(bf16[48,1024]{1,0:T(8,128)(2,1)} %own_far.1), channel_id=1, source_target_pairs={{0,4},{2,6},{4,12},{6,14},{8,0},{10,2},{12,20},{14,22},{16,8},{18,... | collective-permute-start | bytes 294920 | tf_op jit(solution)/shard_map/ppermute | solution.py:390
  3.0 7.4 %collective-permute-start.2 = (bf16[48,1024]{1,0:T(8,128)(2,1)}, bf16[48,1024]{1,0:T(8,128)(2,1)S(1)}, u32[]{:S(2)}, u32[]{:S(2)}) collective-permute-start(bf16[48,1024]{1,0:T(8,128)(2,1)} %own_far.1), channel_id=1, source_target_pairs={{0,2},{2,0},{4,6},{6,4},{8,10},{10,8},{12,14},{14,12},{16,18},{18,... | collective-permute-start | bytes 294920 | tf_op jit(solution)/shard_map/ppermute | solution.py:372
  3.0 7.4 %copy-start = (bf16[128,4096]{1,0:T(8,128)(2,1)S(1)}, bf16[128,4096]{1,0:T(8,128)(2,1)}, u32[]{:S(2)}) copy-start(bf16[128,4096]{1,0:T(8,128)(2,1)} %queries_far.1) | copy-start | bytes 3145732
  3.0 7.4 %copy-start.1 = (bf16[48,1024]{1,0:T(8,128)(2,1)S(1)}, bf16[48,1024]{1,0:T(8,128)(2,1)}, u32[]{:S(2)}) copy-start(bf16[48,1024]{1,0:T(8,128)(2,1)} %own_far.1) | copy-start | bytes 294916
  3.0 7.4 %copy-start.2 = (bf16[1024]{0:T(1024)(128)(2,1)S(1)}, bf16[1024]{0:T(1024)(128)(2,1)}, u32[]{:S(2)}) copy-start(bf16[1024]{0:T(1024)(128)(2,1)} %gain_far.1) | copy-start | bytes 6148
  3.1 7.4 %copy-start.3 = (s32[3]{0:T(128)S(1)}, s32[3]{0:T(128)}, u32[]{:S(2)}) copy-start(s32[3]{0:T(128)} %length_far.1) | copy-start | bytes 40
  7.9 6.0 %collective-permute-start.4 = (bf16[48,1024]{1,0:T(8,128)(2,1)S(1)}, bf16[48,1024]{1,0:T(8,128)(2,1)S(1)}, u32[]{:S(2)}, u32[]{:S(2)}) collective-permute-start(bf16[48,1024]{1,0:T(8,128)(2,1)S(1)} %collective-permute-done.refs_0_), channel_id=1, source_target_pairs={{0,8},{2,10},{4,0},{6,2},{8,16},{10,18},{12,4},{14,6},{16,24},{18,... | collective-permute-start | bytes 294920 | tf_op jit(solution)/shard_map/ppermute | solution.py:389
  9.4 4.6 %collective-permute-start.5 = (bf16[48,1024]{1,0:T(8,128)(2,1)S(1)}, bf16[48,1024]{1,0:T(8,128)(2,1)S(1)}, u32[]{:S(2)}, u32[]{:S(2)}) collective-permute-start(bf16[48,1024]{1,0:T(8,128)(2,1)S(1)} %collective-permute-done.1.refs_1_), channel_id=1, source_target_pairs={{0,4},{2,6},{4,12},{6,14},{8,0},{10,2},{12,20},{14,22},{16,8},{18,... | collective-permute-start | bytes 294920 | tf_op jit(solution)/shard_map/ppermute | solution.py:390
  9.9 5.8 %collective-permute-start.10 = (bf16[48,1024]{1,0:T(8,128)(2,1)S(1)}, bf16[48,1024]{1,0:T(8,128)(2,1)S(1)}, u32[]{:S(2)}, u32[]{:S(2)}) collective-permute-start(bf16[48,1024]{1,0:T(8,128)(2,1)S(1)} %collective-permute-done.refs_0_), channel_id=1, source_target_pairs={{0,2},{2,0},{4,6},{6,4},{8,10},{10,8},{12,14},{14,12},{16,18},{18,... | collective-permute-start | bytes 294920 | tf_op jit(solution)/shard_map/ppermute | solution.py:372
  9.9 6.2 %collective-permute-start.11 = (bf16[48,1024]{1,0:T(8,128)(2,1)S(1)}, bf16[48,1024]{1,0:T(8,128)(2,1)S(1)}, u32[]{:S(2)}, u32[]{:S(2)}) collective-permute-start(bf16[48,1024]{1,0:T(8,128)(2,1)S(1)} %collective-permute-done.1.refs_1_), channel_id=1, source_target_pairs={{0,2},{2,0},{4,6},{6,4},{8,10},{10,8},{12,14},{14,12},{16,18},{18,... | collective-permute-start | bytes 294920 | tf_op jit(solution)/shard_map/ppermute | solution.py:372
  13.7 14.2 %collective-permute-start.3 = (bf16[128,2048]{1,0:T(8,128)(2,1)S(1)}, bf16[128,2048]{1,0:T(8,128)(2,1)S(1)}, u32[]{:S(2)}, u32[]{:S(2)}) collective-permute-start(bf16[128,2048]{1,0:T(8,128)(2,1)S(1)} %get-tuple-element.43), channel_id=1, source_target_pairs={{0,2},{2,0},{4,6},{6,4},{8,10},{10,8},{12,14},{14,12},{16,18},{18,... | collective-permute-start | bytes 1572872 | tf_op jit(solution)/shard_map/ppermute | solution.py:372
  14.0 5.9 %collective-permute-start.8 = (bf16[48,1024]{1,0:T(8,128)(2,1)S(1)}, bf16[48,1024]{1,0:T(8,128)(2,1)S(1)}, u32[]{:S(2)}, u32[]{:S(2)}) collective-permute-start(bf16[48,1024]{1,0:T(8,128)(2,1)S(1)} %collective-permute-done.4.refs_4_), channel_id=1, source_target_pairs={{0,8},{2,10},{4,0},{6,2},{8,16},{10,18},{12,4},{14,6},{16,24},{18,... | collective-permute-start | bytes 294920 | tf_op jit(solution)/shard_map/ppermute | solution.py:389
  15.6 5.7 %collective-permute-start.6 = (bf16[48,1024]{1,0:T(8,128)(2,1)S(1)}, bf16[48,1024]{1,0:T(8,128)(2,1)S(1)}, u32[]{:S(2)}, u32[]{:S(2)}) collective-permute-start(bf16[48,1024]{1,0:T(8,128)(2,1)S(1)} %collective-permute-done.4.refs_4_), channel_id=1, source_target_pairs={{0,2},{2,0},{4,6},{6,4},{8,10},{10,8},{12,14},{14,12},{16,18},{18,... | collective-permute-start | bytes 294920 | tf_op jit(solution)/shard_map/ppermute | solution.py:372
  15.6 5.2 %collective-permute-start.9 = (bf16[48,1024]{1,0:T(8,128)(2,1)S(1)}, bf16[48,1024]{1,0:T(8,128)(2,1)S(1)}, u32[]{:S(2)}, u32[]{:S(2)}) collective-permute-start(bf16[48,1024]{1,0:T(8,128)(2,1)S(1)} %collective-permute-done.5.refs_5_), channel_id=1, source_target_pairs={{0,4},{2,6},{4,12},{6,14},{8,0},{10,2},{12,20},{14,22},{16,8},{18,... | collective-permute-start | bytes 294920 | tf_op jit(solution)/shard_map/ppermute | solution.py:390
  16.1 6.8 %collective-permute-start.7 = (bf16[48,1024]{1,0:T(8,128)(2,1)S(1)}, bf16[48,1024]{1,0:T(8,128)(2,1)S(1)}, u32[]{:S(2)}, u32[]{:S(2)}) collective-permute-start(bf16[48,1024]{1,0:T(8,128)(2,1)S(1)} %collective-permute-done.5.refs_5_), channel_id=1, source_target_pairs={{0,2},{2,0},{4,6},{6,4},{8,10},{10,8},{12,14},{14,12},{16,18},{18,... | collective-permute-start | bytes 294920 | tf_op jit(solution)/shard_map/ppermute | solution.py:372
  20.8 2.0 %collective-permute-start.12 = (bf16[48,1024]{1,0:T(8,128)(2,1)S(1)}, bf16[48,1024]{1,0:T(8,128)(2,1)S(1)}, u32[]{:S(2)}, u32[]{:S(2)}) collective-permute-start(bf16[48,1024]{1,0:T(8,128)(2,1)S(1)} %collective-permute-done.8.refs_2_), channel_id=1, source_target_pairs={{0,2},{2,0},{4,6},{6,4},{8,10},{10,8},{12,14},{14,12},{16,18},{18,... | collective-permute-start | bytes 294920 | tf_op jit(solution)/shard_map/ppermute | solution.py:372
  20.8 2.0 %collective-permute-start.13 = (bf16[48,1024]{1,0:T(8,128)(2,1)S(1)}, bf16[48,1024]{1,0:T(8,128)(2,1)S(1)}, u32[]{:S(2)}, u32[]{:S(2)}) collective-permute-start(bf16[48,1024]{1,0:T(8,128)(2,1)S(1)} %collective-permute-done.9.refs_3_), channel_id=1, source_target_pairs={{0,2},{2,0},{4,6},{6,4},{8,10},{10,8},{12,14},{14,12},{16,18},{18,... | collective-permute-start | bytes 294920 | tf_op jit(solution)/shard_map/ppermute | solution.py:372
  21.4 4.7 %collective-permute-start.14 = (bf16[48,1024]{1,0:T(8,128)(2,1)S(1)}, bf16[48,1024]{1,0:T(8,128)(2,1)S(1)}, u32[]{:S(2)}, u32[]{:S(2)}) collective-permute-start(bf16[48,1024]{1,0:T(8,128)(2,1)S(1)} %collective-permute-done.8.refs_2_), channel_id=1, source_target_pairs={{0,8},{2,10},{4,0},{6,2},{8,16},{10,18},{12,4},{14,6},{16,24},{18,... | collective-permute-start | bytes 294920 | tf_op jit(solution)/shard_map/ppermute | solution.py:389
  22.9 5.0 %collective-permute-start.15 = (bf16[48,1024]{1,0:T(8,128)(2,1)S(1)}, bf16[48,1024]{1,0:T(8,128)(2,1)S(1)}, u32[]{:S(2)}, u32[]{:S(2)}) collective-permute-start(bf16[48,1024]{1,0:T(8,128)(2,1)S(1)} %collective-permute-done.9.refs_3_), channel_id=1, source_target_pairs={{0,6},{2,4},{4,14},{6,12},{8,2},{10,0},{12,22},{14,20},{16,10},{18... | collective-permute-start | bytes 294920 | tf_op jit(solution)/shard_map/ppermute | solution.py:390
  34.8 1.6 %collective-permute-start.16 = (bf16[128,1024]{1,0:T(8,128)(2,1)S(1)}, bf16[128,1024]{1,0:T(8,128)(2,1)S(1)}, u32[]{:S(2)}, u32[]{:S(2)}) collective-permute-start(bf16[128,1024]{1,0:T(8,128)(2,1)S(1)} %get-tuple-element.68), channel_id=1, source_target_pairs={{0,2},{2,0},{4,6},{6,4},{8,10},{10,8},{12,14},{14,12},{16,18},{18,... | collective-permute-start | bytes 786440 | tf_op jit(solution)/shard_map/ppermute | solution.py:372
  36.4 8.4 %collective-permute-start.17 = (bf16[128,1024]{1,0:T(8,128)(2,1)S(1)}, bf16[128,1024]{1,0:T(8,128)(2,1)S(1)}, u32[]{:S(2)}, u32[]{:S(2)}) collective-permute-start(bf16[128,1024]{1,0:T(8,128)(2,1)S(1)} %add_convert_fusion.1), channel_id=1, source_target_pairs={{0,1},{1,0},{2,3},{3,2},{4,5},{5,4},{6,7},{7,6},{8,9},{9,8},{10,11... | collective-permute-start | bytes 786440 | tf_op jit(solution)/shard_map/ppermute | solution.py:424
where the time goes:
time: 44.8 us; the launch traced here: 45.6 us
  Pallas kernels  18.8 us (42%)
  waiting for transfers between devices  14.2 us (32%)
  starting transfers between devices  11.6 us (26%)
  other arithmetic  0.84 us (2%)
    ppermute x4, starting transfers between devices, on_device(): ahead = lax.ppermute(ahead, 'rows', hop(1))  7.7 us
    ppermute x1, waiting for transfers between devices, on_device(): given = lax.ppermute(share, 'heads', turn)  6.86 us
    pallas_call x1, Pallas kernels, attend(): pl.pallas_call(functools.partial(attend_kernel, layout, first, len(pieces...  6.84 us
    pallas_call x2, Pallas kernels, project(): pl.pallas_call(functools.partial(project_kernel, layout, first, len(piece...  6.35 us
    ppermute x4, waiting for transfers between devices, on_device(): lax.ppermute(behind, 'rows', hop(-1, 1 if len(sources) == 2 else 0))  4.86 us
    pallas_call x1, Pallas kernels, begin(): pl.pallas_call(functools.partial(begin_kernel, layout, chips), in_specs=[...  3.31 us
    pallas_call x1, Pallas kernels, stage(): pl.pallas_call(functools.partial(stage_kernel, axis), in_specs=[SCALARS,...  2.29 us
    ppermute x1, starting transfers between devices, on_device(): given = lax.ppermute(share, 'heads', turn)  1.55 us
  transfers between devices with their start and end apart: 18, of which 8 were waited for; matrix products, arithmetic and copies ran while one was open for 0% of the time, Pallas kernels for 26%

commit v1 on v0

--- a/solution.py
+++ b/solution.py
@@ -11,6 +11,7 @@
 PASS_LEN = 256
 LOWEST = -1e30
 TILE = 16
+TAIL_PARTS = 2
 WIDE = 1024
 ON_CHIP = pl.BlockSpec(memory_space=pltpu.VMEM)
 SCALARS = pl.BlockSpec(memory_space=pltpu.SMEM)
@@ -272,7 +273,8 @@
 def attend_kernel(layout, first, count, cases, plan, gain_ref, key_w_ref, value_w_ref, mask, own_q_ref, other_q_ref,
                   out_w_ref, *refs):
     piece_refs = refs[:count]
-    own_ref, other_ref, keys_ref, values_ref, raw, rows = refs[count + 2:]
+    result_refs = refs[count + 2: -4]
+    keys_ref, values_ref, raw, rows = refs[-4:]
     append(layout, first, cases_of(raw.shape[0]), plan, piece_refs, gain_ref, key_w_ref, value_w_ref,
            keys_ref, values_ref, raw, rows)
     half, inner = own_q_ref.shape
@@ -322,8 +324,9 @@
         product = jnp.dot(
             jnp.concatenate(attended, axis=1), out_w_ref[...], preferred_element_type=jnp.float32
         )
-        own_ref[...] = product[:half, :].astype(jnp.bfloat16)
-        other_ref[...] = product[half:, :].astype(jnp.bfloat16)
+        part = result_refs[0].shape[0]
+        for index, result_ref in enumerate(result_refs):
+            result_ref[...] = product[index * part:(index + 1) * part, :].astype(jnp.bfloat16)
 
     low = 0
     for number in cases:
@@ -336,21 +339,21 @@
     width = out_w.shape[1]
     enc_rows = layout.tiles * TILE
     cases = [enc_rows * 2 // 3 // 64 * 64, enc_rows]
-    result = jax.ShapeDtypeStruct((rows_here, width), jnp.bfloat16)
+    result = jax.ShapeDtypeStruct((rows_here // TAIL_PARTS, width), jnp.bfloat16)
     kept = jax.ShapeDtypeStruct(held[0].shape, jnp.bfloat16)
     at = 8 + len(pieces)
-    own, other, _, _ = pl.pallas_call(
+    *results, _, _ = pl.pallas_call(
         functools.partial(attend_kernel, layout, first, len(pieces), cases),
         in_specs=[SCALARS] + [ON_CHIP] * (at + 1),
-        out_specs=[ON_CHIP] * 4,
-        out_shape=[result, result, kept, kept],
+        out_specs=[ON_CHIP] * (2 * TAIL_PARTS + 2),
+        out_shape=[result] * (2 * TAIL_PARTS) + [kept, kept],
         scratch_shapes=[pltpu.VMEM((len(pieces) * layout.rows_piece, width), jnp.bfloat16)] * 2,
-        input_output_aliases={at: 2, at + 1: 3},
+        input_output_aliases={at: 2 * TAIL_PARTS, at + 1: 2 * TAIL_PARTS + 1},
         compiler_params=params(24),
         cost_estimate=cost(4 * rows_here * (2 * enc_rows + width) * half, 2 * half * width),
         name="attend",
     )(plan, gain, key_w, value_w, mask, own_q, other_q, out_w, *pieces, *held)
-    return own, other
+    return results[:TAIL_PARTS], results[TAIL_PARTS:]
 
 
 def on_device(number, queries, passages, enc_gain, key_weight, value_weight, out_weight, passage_length):
@@ -390,7 +393,7 @@
         behind = lax.ppermute(behind, "rows", hop(-1, 1 if len(sources) == 2 else 0))
         if index == 0:
             key_w = stage(device, key_weight, 1)
-            ahead, behind, key_w = lax.optimization_barrier((ahead, behind, key_w))
+            ahead, key_w = lax.optimization_barrier((ahead, key_w))
         if index == min(1, len(rounds) - 1):
             plan, gain, value_w, keys, values, own_q, given_q, mask = begin(
                 layout, chips, device, passage_length, enc_gain, key_w, value_weight,
@@ -408,7 +411,7 @@
             else:
                 held.append(staged)
             first, waiting = first + now, waiting[now:]
-        ahead, behind, *held = lax.optimization_barrier((ahead, behind, *held))
+        ahead, *held = lax.optimization_barrier((ahead, *held))
         waiting = waiting + ([ahead, behind] if len(sources) == 2 else [ahead, behind, cross(ahead), cross(behind)])
     if out_w is None:
         out_w = stage(device, out_weight, 0)
@@ -417,14 +420,21 @@
     own, other = attend(
         layout, first, plan, gain, key_w, value_w, mask, own_q, other_q, out_w, waiting, held
     )
-    share = (own.astype(jnp.float32) + cross(other).astype(jnp.float32)).astype(jnp.bfloat16)
+    received = [cross(part) for part in other]
+    shares = [
+        (ours.astype(jnp.float32) + theirs.astype(jnp.float32)).astype(jnp.bfloat16)
+        for ours, theirs in zip(own, received)
+    ]
     by = 1
     while by < heads_axis:
         turn = [(place, place ^ by) for place in range(heads_axis)]
-        given = lax.ppermute(share, "heads", turn)
-        share = (share.astype(jnp.float32) + given.astype(jnp.float32)).astype(jnp.bfloat16)
+        given = [lax.ppermute(share, "heads", turn) for share in shares]
+        shares = [
+            (ours.astype(jnp.float32) + theirs.astype(jnp.float32)).astype(jnp.bfloat16)
+            for ours, theirs in zip(shares, given)
+        ]
         by *= 2
-    return share
+    return jnp.concatenate(shares, axis=0)
 
 
 def solution(mesh):

time: 44.8 us -> 42.6 us (0.951); the launches traced: 45.6 us -> 42.4 us
  waiting for transfers between devices: 14.2 us -> 10.7 us
  starting transfers between devices: 11.6 us -> 12.9 us
  Pallas kernels: 18.8 us -> 17.8 us
    ppermute x4, waiting for transfers between devices: 4.86 us -> 2.49 us  [on_device(): lax.ppermute(behind, 'rows', hop(-1, 1 if len(sources) == 2 else 0))]
    concatenate x0 -> x1, other arithmetic: none -> 0.72 us  [on_device(): return jnp.concatenate(shares, axis=0)]
    convert_element_type x2 -> x4, other arithmetic: 0.84 us -> 0.14 us  [on_device(): (ours.astype(jnp.float32) + theirs.astype(jnp.float32)).astype(jnp.bfloat16)]
    ppermute x1 -> x2, waiting for transfers between devices: 6.86 us -> 6.18 us  [on_device(): given = [lax.ppermute(share, 'heads', turn) for share in shares]]
    ppermute x4, starting transfers between devices: 7.7 us -> 8.34 us  [on_device(): ahead = lax.ppermute(ahead, 'rows', hop(1))]
    ppermute x9 -> x10, waiting for transfers between devices: 1.49 us -> 0.86 us  [cross(): return lax.ppermute(piece, 'rows', other_core)]
    ppermute x1 -> x2, starting transfers between devices: 1.55 us -> 2.16 us  [on_device(): given = [lax.ppermute(share, 'heads', turn) for share in shares]]
    pallas_call x2, Pallas kernels: 6.35 us -> 5.76 us  [project(): pl.pallas_call(functools.partial(project_kernel, layout, first, len(piece...]
  transfers between devices with their start and end apart: 18 -> 20, of which waited for: 8 -> 7; matrix products, arithmetic and copies ran while one was open for 0% -> 0% of each run, Pallas kernels for 26% -> 27%
where the time goes in v1:
time: 42.6 us; the launch traced here: 42.4 us
  Pallas kernels  17.8 us (42%)
  starting transfers between devices  12.9 us (30%)
  waiting for transfers between devices  10.7 us (25%)
  other arithmetic  0.86 us (2%)
    ppermute x4, starting transfers between devices, on_device(): ahead = lax.ppermute(ahead, 'rows', hop(1))  8.34 us
    pallas_call x1, Pallas kernels, attend(): pl.pallas_call(functools.partial(attend_kernel, layout, first, len(pieces...  6.4 us
    ppermute x2, waiting for transfers between devices, on_device(): given = [lax.ppermute(share, 'heads', turn) for share in shares]  6.18 us
    pallas_call x2, Pallas kernels, project(): pl.pallas_call(functools.partial(project_kernel, layout, first, len(piece...  5.76 us
    pallas_call x1, Pallas kernels, begin(): pl.pallas_call(functools.partial(begin_kernel, layout, chips), in_specs=[...  3.3 us
    ppermute x4, waiting for transfers between devices, on_device(): lax.ppermute(behind, 'rows', hop(-1, 1 if len(sources) == 2 else 0))  2.49 us
    pallas_call x1, Pallas kernels, stage(): pl.pallas_call(functools.partial(stage_kernel, axis), in_specs=[SCALARS,...  2.29 us
    ppermute x2, starting transfers between devices, on_device(): given = [lax.ppermute(share, 'heads', turn) for share in shares]  2.16 us
  transfers between devices with their start and end apart: 20, of which 7 were waited for; matrix products, arithmetic and copies ran while one was open for 0% of the time, Pallas kernels for 27%

profile of v1, /device:TPU:0, one launch (start us, length us, event | category | flops | bytes accessed | tf_op | source)
XLA Modules:
  0.0 42.4 jit_solution(8396248772989188743)
XLA Ops:
  0.0 3.0 %collective-permute-start = (bf16[48,1024]{1,0:T(8,128)(2,1)}, bf16[48,1024]{1,0:T(8,128)(2,1)S(1)}, u32[]{:S(2)}, u32[]{:S(2)}) collective-permute-start(bf16[48,1024]{1,0:T(8,128)(2,1)} %own_far.1), channel_id=1, source_target_pairs={{0,8},{2,10},{4,0},{6,2},{8,16},{10,18},{12,4},{14,6},{16,24},{18,... | collective-permute-start | bytes 294920 | tf_op jit(solution)/shard_map/ppermute | solution.py:392
  3.0 0.0 collective-permute-start.5
  3.0 0.0 collective-permute-start.1
  3.1 2.3 %stage.1.key_w_ref = bf16[1024,2048]{1,0:T(8,128)(2,1)S(1)} custom-call(s32[1]{0:T(128)} %bitcast.device_ref, bf16[1024,4096]{1,0:T(8,128)(2,1)} %far.1), custom_call_target="tpu_custom_call" | custom-call | bytes 8388608 | tf_op jit(solution)/shard_map/stage/pallas_call | solution.py:122
  5.4 0.6 %collective-permute-done.refs_0_ = bf16[48,1024]{1,0:T(8,128)(2,1)S(1)} collective-permute-done((bf16[48,1024]{1,0:T(8,128)(2,1)}, bf16[48,1024]{1,0:T(8,128)(2,1)S(1)}, u32[]{:S(2)}, u32[]{:S(2)}) %collective-permute-start) | collective-permute-done | bytes 98336 | tf_op jit(solution)/shard_map/ppermute | solution.py:392
  6.0 1.9 %collective-permute-start.3 = (bf16[48,1024]{1,0:T(8,128)(2,1)S(1)}, bf16[48,1024]{1,0:T(8,128)(2,1)S(1)}, u32[]{:S(2)}, u32[]{:S(2)}) collective-permute-start(bf16[48,1024]{1,0:T(8,128)(2,1)S(1)} %collective-permute-done.refs_0_), channel_id=1, source_target_pairs={{0,8},{2,10},{4,0},{6,2},{8,16},{10,18},{12,4},{14,6},{16,24},{18,... | collective-permute-start | bytes 294920 | tf_op jit(solution)/shard_map/ppermute | solution.py:392
  7.9 0.1 collective-permute-start.6
  8.0 0.4 collective-permute-start.10
  8.4 3.3 %begin.1 = (s32[101]{0:T(128)S(1)}, bf16[1024]{0:T(1024)(128)(2,1)S(1)}, bf16[1024,2048]{1,0:T(8,128)(2,1)S(1)}, bf16[768,2048]{1,0:T(8,128)(2,1)S(1)}, bf16[768...) custom-call(s32[1]{0:T(128)} %bitcast.device_ref, ...), custom_call_target="tpu_custom_call" | custom-call | flops 805306368 | bytes 16777216 | tf_op jit(solution)/shard_map/begin/pallas_call | solution.py:189
  11.7 0.2 collective-permute-start.2
  11.9 0.0 collective-permute-done.3.refs_4_
  11.9 1.9 %collective-permute-start.8 = (bf16[48,1024]{1,0:T(8,128)(2,1)S(1)}, bf16[48,1024]{1,0:T(8,128)(2,1)S(1)}, u32[]{:S(2)}, u32[]{:S(2)}) collective-permute-start(bf16[48,1024]{1,0:T(8,128)(2,1)S(1)} %collective-permute-done.3.refs_4_), channel_id=1, source_target_pairs={{0,8},{2,10},{4,0},{6,2},{8,16},{10,18},{12,4},{14,6},{16,24},{18,... | collective-permute-start | bytes 294920 | tf_op jit(solution)/shard_map/ppermute | solution.py:392
  13.8 0.0 collective-permute-start.4
  13.8 0.2 collective-permute-start.11
  14.1 0.3 collective-permute-start.7
  14.4 3.0 %project.2 = (bf16[768,2048]{1,0:T(8,128)(2,1)S(1)}, bf16[768,2048]{1,0:T(8,128)(2,1)S(1)}) custom-call(s32[101]{0:T(128)S(1)} %get-tuple-element.34.plan, bf16[1024]{0:T(1024)(128)(2,1)S(1)} %get-tuple-element.35.gain_ref, bf16[1024,2048]{1,0:T(8,128)(2,1)S(1)} %stage.1.key_w_ref, ...), custom_call_target="tpu_custom_call", output_to_operand_aliasing={{0}: (10, {}), {1}: (11, {})} | custom-call | flops 2415919104 | bytes 8388608 | tf_op jit(solution)/shard_map/project/pallas_call | solution.py:260
  17.4 0.2 collective-permute-start.12
  17.7 1.4 %collective-permute-done.11.refs_3_ = bf16[48,1024]{1,0:T(8,128)(2,1)S(1)} collective-permute-done((bf16[48,1024]{1,0:T(8,128)(2,1)S(1)}, bf16[48,1024]{1,0:T(8,128)(2,1)S(1)}, u32[]{:S(2)}, u32[]{:S(2)}) %collective-permute-start.11) | collective-permute-done | bytes 98336 | tf_op jit(solution)/shard_map/ppermute | solution.py:393
  19.0 1.6 %collective-permute-start.14 = (bf16[48,1024]{1,0:T(8,128)(2,1)S(1)}, bf16[48,1024]{1,0:T(8,128)(2,1)S(1)}, u32[]{:S(2)}, u32[]{:S(2)}) collective-permute-start(bf16[48,1024]{1,0:T(8,128)(2,1)S(1)} %collective-permute-done.8.refs_2_), channel_id=1, source_target_pairs={{0,8},{2,10},{4,0},{6,2},{8,16},{10,18},{12,4},{14,6},{16,24},{18,... | collective-permute-start | bytes 294920 | tf_op jit(solution)/shard_map/ppermute | solution.py:392
  20.6 0.3 collective-permute-start.15
  20.9 2.7 %project.3 = (bf16[768,2048]{1,0:T(8,128)(2,1)S(1)}, bf16[768,2048]{1,0:T(8,128)(2,1)S(1)}, bf16[2048,1024]{1,0:T(8,128)(2,1)S(1)}) custom-call(s32[101]{0:T(128)S(1)} %get-tuple-element.34.plan, bf16[1024]{0:T(1024)(128)(2,1)S(1)} %get-tuple-element.35.gain_ref, ...), custom_call_target="tpu_custom_call", output_to_operand_aliasing={{0}: (11, {}), {1}: (12, {})} | custom-call | flops 2415919104 | bytes 8388608 | tf_op jit(solution)/shard_map/project/pallas_call | solution.py:260
  23.7 0.6 %collective-permute-done.14.refs_0_ = bf16[48,1024]{1,0:T(8,128)(2,1)S(1)} collective-permute-done((bf16[48,1024]{1,0:T(8,128)(2,1)S(1)}, bf16[48,1024]{1,0:T(8,128)(2,1)S(1)}, u32[]{:S(2)}, u32[]{:S(2)}) %collective-permute-start.14) | collective-permute-done | bytes 98336 | tf_op jit(solution)/shard_map/ppermute | solution.py:392
  24.2 1.1 %collective-permute-done.15.refs_1_ = bf16[48,1024]{1,0:T(8,128)(2,1)S(1)} collective-permute-done((bf16[48,1024]{1,0:T(8,128)(2,1)S(1)}, bf16[48,1024]{1,0:T(8,128)(2,1)S(1)}, u32[]{:S(2)}, u32[]{:S(2)}) %collective-permute-start.15) | collective-permute-done | bytes 98336 | tf_op jit(solution)/shard_map/ppermute | solution.py:393
  25.4 6.4 %attend.1 = (bf16[64,1024]{1,0:T(8,128)(2,1)S(1)}, bf16[64,1024]{1,0:T(8,128)(2,1)S(1)}, bf16[64,1024]{1,0:T(8,128)(2,1)S(1)}, bf16[64,1024]{1,0:T(8,128)(2,1)S(...) custom-call(s32[101]{0:T(128)S(1)} %get-tuple-element.34.plan, ...), custom_call_target="tpu_custom_call", output_to_operand_aliasing={{4}: (10, {}), {5}: (11, {})} | custom-call | flops 2684354560 | bytes 4194304 | tf_op jit(solution)/shard_map/attend/pallas_call | solution.py:345
  31.8 0.2 collective-permute-start.16
  32.0 0.4 collective-permute-start.18
  32.4 0.8 %collective-permute-done.16 = bf16[64,1024]{1,0:T(8,128)(2,1)S(1)} collective-permute-done((bf16[64,1024]{1,0:T(8,128)(2,1)S(1)}, bf16[64,1024]{1,0:T(8,128)(2,1)S(1)}, u32[]{:S(2)}, u32[]{:S(2)}) %collective-permute-start.16) | collective-permute-done | bytes 131104 | tf_op jit(solution)/shard_map/ppermute | solution.py:375
  33.2 1.6 %collective-permute-start.17 = (bf16[64,1024]{1,0:T(8,128)(2,1)S(1)}, bf16[64,1024]{1,0:T(8,128)(2,1)S(1)}, u32[]{:S(2)}, u32[]{:S(2)}) collective-permute-start(bf16[64,1024]{1,0:T(8,128)(2,1)S(1)} %add_convert_fusion.3), channel_id=1, source_target_pairs={{0,1},{1,0},{2,3},{3,2},{4,5},{5,4},{6,7},{7,6},{8,9},{9,8},{10,11... | collective-permute-start | bytes 393224 | tf_op jit(solution)/shard_map/ppermute | solution.py:431
  34.8 0.6 %collective-permute-start.19 = (bf16[64,1024]{1,0:T(8,128)(2,1)S(1)}, bf16[64,1024]{1,0:T(8,128)(2,1)S(1)}, u32[]{:S(2)}, u32[]{:S(2)}) collective-permute-start(bf16[64,1024]{1,0:T(8,128)(2,1)S(1)} %add_convert_fusion.1), channel_id=1, source_target_pairs={{0,1},{1,0},{2,3},{3,2},{4,5},{5,4},{6,7},{7,6},{8,9},{9,8},{10,11... | collective-permute-start | bytes 393224 | tf_op jit(solution)/shard_map/ppermute | solution.py:431
  35.4 4.2 %collective-permute-done.17 = bf16[64,1024]{1,0:T(8,128)(2,1)S(1)} collective-permute-done((bf16[64,1024]{1,0:T(8,128)(2,1)S(1)}, bf16[64,1024]{1,0:T(8,128)(2,1)S(1)}, u32[]{:S(2)}, u32[]{:S(2)}) %collective-permute-start.17) | collective-permute-done | bytes 131104 | tf_op jit(solution)/shard_map/ppermute | solution.py:431
  39.7 2.0 %collective-permute-done.19 = bf16[64,1024]{1,0:T(8,128)(2,1)S(1)} collective-permute-done((bf16[64,1024]{1,0:T(8,128)(2,1)S(1)}, bf16[64,1024]{1,0:T(8,128)(2,1)S(1)}, u32[]{:S(2)}, u32[]{:S(2)}) %collective-permute-start.19) | collective-permute-done | bytes 131104 | tf_op jit(solution)/shard_map/ppermute | solution.py:431
  41.7 0.7 %pad_maximum_fusion = bf16[128,1024]{1,0:T(8,128)(2,1)} fusion(bf16[64,1024]{1,0:T(8,128)(2,1)S(1)} %add_convert_fusion, bf16[64,1024]{1,0:T(8,128)(2,1)S(1)} %add_convert_fusion.2), kind=kLoop, calls=%fused_computation | loop fusion | flops 524288 | bytes 524288 | tf_op jit(solution)/shard_map/concatenate | solution.py:437
  (26 shorter events, 0.2 us)
Async XLA Ops:
  0.0 6.0 %collective-permute-start = (bf16[48,1024]{1,0:T(8,128)(2,1)}, bf16[48,1024]{1,0:T(8,128)(2,1)S(1)}, u32[]{:S(2)}, u32[]{:S(2)}) collective-permute-start(bf16[48,1024]{1,0:T(8,128)(2,1)} %own_far.1), channel_id=1, source_target_pairs={{0,8},{2,10},{4,0},{6,2},{8,16},{10,18},{12,4},{14,6},{16,24},{18,... | collective-permute-start | bytes 294920 | tf_op jit(solution)/shard_map/ppermute | solution.py:392
  3.0 4.8 %collective-permute-start.5 = (bf16[48,1024]{1,0:T(8,128)(2,1)}, bf16[48,1024]{1,0:T(8,128)(2,1)S(1)}, u32[]{:S(2)}, u32[]{:S(2)}) collective-permute-start(bf16[48,1024]{1,0:T(8,128)(2,1)} %own_far.1), channel_id=1, source_target_pairs={{0,4},{2,6},{4,12},{6,14},{8,0},{10,2},{12,20},{14,22},{16,8},{18,... | collective-permute-start | bytes 294920 | tf_op jit(solution)/shard_map/ppermute | solution.py:393
  3.0 5.3 %collective-permute-start.1 = (bf16[48,1024]{1,0:T(8,128)(2,1)}, bf16[48,1024]{1,0:T(8,128)(2,1)S(1)}, u32[]{:S(2)}, u32[]{:S(2)}) collective-permute-start(bf16[48,1024]{1,0:T(8,128)(2,1)} %own_far.1), channel_id=1, source_target_pairs={{0,2},{2,0},{4,6},{6,4},{8,10},{10,8},{12,14},{14,12},{16,18},{18,... | collective-permute-start | bytes 294920 | tf_op jit(solution)/shard_map/ppermute | solution.py:375
  3.0 5.3 %copy-start = (bf16[128,4096]{1,0:T(8,128)(2,1)S(1)}, bf16[128,4096]{1,0:T(8,128)(2,1)}, u32[]{:S(2)}) copy-start(bf16[128,4096]{1,0:T(8,128)(2,1)} %queries_far.1) | copy-start | bytes 3145732
  3.0 5.3 %copy-start.1 = (bf16[48,1024]{1,0:T(8,128)(2,1)S(1)}, bf16[48,1024]{1,0:T(8,128)(2,1)}, u32[]{:S(2)}) copy-start(bf16[48,1024]{1,0:T(8,128)(2,1)} %own_far.1) | copy-start | bytes 294916
  3.0 5.3 %copy-start.2 = (bf16[1024]{0:T(1024)(128)(2,1)S(1)}, bf16[1024]{0:T(1024)(128)(2,1)}, u32[]{:S(2)}) copy-start(bf16[1024]{0:T(1024)(128)(2,1)} %gain_far.1) | copy-start | bytes 6148
  3.1 5.3 %copy-start.3 = (s32[3]{0:T(128)S(1)}, s32[3]{0:T(128)}, u32[]{:S(2)}) copy-start(s32[3]{0:T(128)} %length_far.1) | copy-start | bytes 40
  6.0 6.0 %collective-permute-start.3 = (bf16[48,1024]{1,0:T(8,128)(2,1)S(1)}, bf16[48,1024]{1,0:T(8,128)(2,1)S(1)}, u32[]{:S(2)}, u32[]{:S(2)}) collective-permute-start(bf16[48,1024]{1,0:T(8,128)(2,1)S(1)} %collective-permute-done.refs_0_), channel_id=1, source_target_pairs={{0,8},{2,10},{4,0},{6,2},{8,16},{10,18},{12,4},{14,6},{16,24},{18,... | collective-permute-start | bytes 294920 | tf_op jit(solution)/shard_map/ppermute | solution.py:392
  7.9 6.0 %collective-permute-start.9 = (bf16[48,1024]{1,0:T(8,128)(2,1)S(1)}, bf16[48,1024]{1,0:T(8,128)(2,1)S(1)}, u32[]{:S(2)}, u32[]{:S(2)}) collective-permute-start(bf16[48,1024]{1,0:T(8,128)(2,1)S(1)} %collective-permute-done.refs_0_), channel_id=1, source_target_pairs={{0,2},{2,0},{4,6},{6,4},{8,10},{10,8},{12,14},{14,12},{16,18},{18,... | collective-permute-start | bytes 294920 | tf_op jit(solution)/shard_map/ppermute | solution.py:375
  7.9 6.0 %collective-permute-start.6 = (bf16[48,1024]{1,0:T(8,128)(2,1)S(1)}, bf16[48,1024]{1,0:T(8,128)(2,1)S(1)}, u32[]{:S(2)}, u32[]{:S(2)}) collective-permute-start(bf16[48,1024]{1,0:T(8,128)(2,1)S(1)} %collective-permute-done.5.refs_1_), channel_id=1, source_target_pairs={{0,4},{2,6},{4,12},{6,14},{8,0},{10,2},{12,20},{14,22},{16,8},{18,... | collective-permute-start | bytes 294920 | tf_op jit(solution)/shard_map/ppermute | solution.py:393
  8.0 6.1 %collective-permute-start.10 = (bf16[48,1024]{1,0:T(8,128)(2,1)S(1)}, bf16[48,1024]{1,0:T(8,128)(2,1)S(1)}, u32[]{:S(2)}, u32[]{:S(2)}) collective-permute-start(bf16[48,1024]{1,0:T(8,128)(2,1)S(1)} %collective-permute-done.5.refs_1_), channel_id=1, source_target_pairs={{0,2},{2,0},{4,6},{6,4},{8,10},{10,8},{12,14},{14,12},{16,18},{18,... | collective-permute-start | bytes 294920 | tf_op jit(solution)/shard_map/ppermute | solution.py:375
  11.7 13.7 %collective-permute-start.2 = (bf16[128,2048]{1,0:T(8,128)(2,1)S(1)}, bf16[128,2048]{1,0:T(8,128)(2,1)S(1)}, u32[]{:S(2)}, u32[]{:S(2)}) collective-permute-start(bf16[128,2048]{1,0:T(8,128)(2,1)S(1)} %get-tuple-element.39), channel_id=1, source_target_pairs={{0,2},{2,0},{4,6},{6,4},{8,10},{10,8},{12,14},{14,12},{16,18},{18,... | collective-permute-start | bytes 1572872 | tf_op jit(solution)/shard_map/ppermute | solution.py:375
  11.9 5.5 %collective-permute-start.8 = (bf16[48,1024]{1,0:T(8,128)(2,1)S(1)}, bf16[48,1024]{1,0:T(8,128)(2,1)S(1)}, u32[]{:S(2)}, u32[]{:S(2)}) collective-permute-start(bf16[48,1024]{1,0:T(8,128)(2,1)S(1)} %collective-permute-done.3.refs_4_), channel_id=1, source_target_pairs={{0,8},{2,10},{4,0},{6,2},{8,16},{10,18},{12,4},{14,6},{16,24},{18,... | collective-permute-start | bytes 294920 | tf_op jit(solution)/shard_map/ppermute | solution.py:392
  13.8 5.2 %collective-permute-start.4 = (bf16[48,1024]{1,0:T(8,128)(2,1)S(1)}, bf16[48,1024]{1,0:T(8,128)(2,1)S(1)}, u32[]{:S(2)}, u32[]{:S(2)}) collective-permute-start(bf16[48,1024]{1,0:T(8,128)(2,1)S(1)} %collective-permute-done.3.refs_4_), channel_id=1, source_target_pairs={{0,2},{2,0},{4,6},{6,4},{8,10},{10,8},{12,14},{14,12},{16,18},{18,... | collective-permute-start | bytes 294920 | tf_op jit(solution)/shard_map/ppermute | solution.py:375
  13.8 5.2 %collective-permute-start.11 = (bf16[48,1024]{1,0:T(8,128)(2,1)S(1)}, bf16[48,1024]{1,0:T(8,128)(2,1)S(1)}, u32[]{:S(2)}, u32[]{:S(2)}) collective-permute-start(bf16[48,1024]{1,0:T(8,128)(2,1)S(1)} %collective-permute-done.6.refs_5_), channel_id=1, source_target_pairs={{0,4},{2,6},{4,12},{6,14},{8,0},{10,2},{12,20},{14,22},{16,8},{18,... | collective-permute-start | bytes 294920 | tf_op jit(solution)/shard_map/ppermute | solution.py:393
  14.1 6.5 %collective-permute-start.7 = (bf16[48,1024]{1,0:T(8,128)(2,1)S(1)}, bf16[48,1024]{1,0:T(8,128)(2,1)S(1)}, u32[]{:S(2)}, u32[]{:S(2)}) collective-permute-start(bf16[48,1024]{1,0:T(8,128)(2,1)S(1)} %collective-permute-done.6.refs_5_), channel_id=1, source_target_pairs={{0,2},{2,0},{4,6},{6,4},{8,10},{10,8},{12,14},{14,12},{16,18},{18,... | collective-permute-start | bytes 294920 | tf_op jit(solution)/shard_map/ppermute | solution.py:375
  17.4 3.5 %collective-permute-start.12 = (bf16[48,1024]{1,0:T(8,128)(2,1)S(1)}, bf16[48,1024]{1,0:T(8,128)(2,1)S(1)}, u32[]{:S(2)}, u32[]{:S(2)}) collective-permute-start(bf16[48,1024]{1,0:T(8,128)(2,1)S(1)} %collective-permute-done.8.refs_2_), channel_id=1, source_target_pairs={{0,2},{2,0},{4,6},{6,4},{8,10},{10,8},{12,14},{14,12},{16,18},{18,... | collective-permute-start | bytes 294920 | tf_op jit(solution)/shard_map/ppermute | solution.py:375
  19.0 1.9 %collective-permute-start.13 = (bf16[48,1024]{1,0:T(8,128)(2,1)S(1)}, bf16[48,1024]{1,0:T(8,128)(2,1)S(1)}, u32[]{:S(2)}, u32[]{:S(2)}) collective-permute-start(bf16[48,1024]{1,0:T(8,128)(2,1)S(1)} %collective-permute-done.11.refs_3_), channel_id=1, source_target_pairs={{0,2},{2,0},{4,6},{6,4},{8,10},{10,8},{12,14},{14,12},{16,18},{18,... | collective-permute-start | bytes 294920 | tf_op jit(solution)/shard_map/ppermute | solution.py:375
  19.0 5.2 %collective-permute-start.14 = (bf16[48,1024]{1,0:T(8,128)(2,1)S(1)}, bf16[48,1024]{1,0:T(8,128)(2,1)S(1)}, u32[]{:S(2)}, u32[]{:S(2)}) collective-permute-start(bf16[48,1024]{1,0:T(8,128)(2,1)S(1)} %collective-permute-done.8.refs_2_), channel_id=1, source_target_pairs={{0,8},{2,10},{4,0},{6,2},{8,16},{10,18},{12,4},{14,6},{16,24},{18,... | collective-permute-start | bytes 294920 | tf_op jit(solution)/shard_map/ppermute | solution.py:392
  20.6 4.8 %collective-permute-start.15 = (bf16[48,1024]{1,0:T(8,128)(2,1)S(1)}, bf16[48,1024]{1,0:T(8,128)(2,1)S(1)}, u32[]{:S(2)}, u32[]{:S(2)}) collective-permute-start(bf16[48,1024]{1,0:T(8,128)(2,1)S(1)} %collective-permute-done.11.refs_3_), channel_id=1, source_target_pairs={{0,6},{2,4},{4,14},{6,12},{8,2},{10,0},{12,22},{14,20},{16,10},{18... | collective-permute-start | bytes 294920 | tf_op jit(solution)/shard_map/ppermute | solution.py:393
  31.8 1.4 %collective-permute-start.16 = (bf16[64,1024]{1,0:T(8,128)(2,1)S(1)}, bf16[64,1024]{1,0:T(8,128)(2,1)S(1)}, u32[]{:S(2)}, u32[]{:S(2)}) collective-permute-start(bf16[64,1024]{1,0:T(8,128)(2,1)S(1)} %get-tuple-element.58), channel_id=1, source_target_pairs={{0,2},{2,0},{4,6},{6,4},{8,10},{10,8},{12,14},{14,12},{16,18},{18,... | collective-permute-start | bytes 393224 | tf_op jit(solution)/shard_map/ppermute | solution.py:375
  32.0 2.8 %collective-permute-start.18 = (bf16[64,1024]{1,0:T(8,128)(2,1)S(1)}, bf16[64,1024]{1,0:T(8,128)(2,1)S(1)}, u32[]{:S(2)}, u32[]{:S(2)}) collective-permute-start(bf16[64,1024]{1,0:T(8,128)(2,1)S(1)} %get-tuple-element.60), channel_id=1, source_target_pairs={{0,2},{2,0},{4,6},{6,4},{8,10},{10,8},{12,14},{14,12},{16,18},{18,... | collective-permute-start | bytes 393224 | tf_op jit(solution)/shard_map/ppermute | solution.py:375
  33.2 6.4 %collective-permute-start.17 = (bf16[64,1024]{1,0:T(8,128)(2,1)S(1)}, bf16[64,1024]{1,0:T(8,128)(2,1)S(1)}, u32[]{:S(2)}, u32[]{:S(2)}) collective-permute-start(bf16[64,1024]{1,0:T(8,128)(2,1)S(1)} %add_convert_fusion.3), channel_id=1, source_target_pairs={{0,1},{1,0},{2,3},{3,2},{4,5},{5,4},{6,7},{7,6},{8,9},{9,8},{10,11... | collective-permute-start | bytes 393224 | tf_op jit(solution)/shard_map/ppermute | solution.py:431
  34.8 6.8 %collective-permute-start.19 = (bf16[64,1024]{1,0:T(8,128)(2,1)S(1)}, bf16[64,1024]{1,0:T(8,128)(2,1)S(1)}, u32[]{:S(2)}, u32[]{:S(2)}) collective-permute-start(bf16[64,1024]{1,0:T(8,128)(2,1)S(1)} %add_convert_fusion.1), channel_id=1, source_target_pairs={{0,1},{1,0},{2,3},{3,2},{4,5},{5,4},{6,7},{7,6},{8,9},{9,8},{10,11... | collective-permute-start | bytes 393224 | tf_op jit(solution)/shard_map/ppermute | solution.py:431
